TPU v7x, 32 devices: a whole 2x2x4 slice. The times are simulated.
32 devices in a mesh: job: 2 (over x), dp: 2 (over core), mp: 8 (over z, y).
Axes of the slice: x: 2, y: 2, z: 4, core: 2. Of those that a mesh axis runs over, the one named last changes fastest.
Arguments:
- output_gradient: bfloat16 [8192, 5120], P(('job', 'dp', 'mp')), parts along dimension 0, may hold values from -6 to 6
- hidden: bfloat16 [8192, 12800], P(('job', 'dp'), 'mp'), parts along dimension 0, may hold values from -6 to 6
- down_weight_frozen: bfloat16 [12800, 5120], P('mp'), may hold values from -0.0546875 to 0.0546875
- adapter_down_maps: bfloat16 [16, 12800, 16], P(None, 'mp'), may hold values from -0.14941406 to 0.14941406
- adapter_up_maps: bfloat16 [16, 16, 5120], P(None, None, 'mp'), may hold values from -0.078125 to 0.078125
- segment_length_list: int32 [4, 16], P(('job', 'dp')), parts along dimension 0, may hold values from 1 to 512, 2048 in all within a row
- segment_adapter_index: int32 [4, 16], P(('job', 'dp')), parts along dimension 0, may hold values from 0 to 15
- owner_slot_adapter: int32 [32], P('job'), parts along dimension 0, may hold values from 0 to 15, as said below
- adapter_token_totals: int32 [32], P('job'), parts along dimension 0, may hold values from 64 to 1023
Outputs:
- grad_hidden: bfloat16 [8192, 12800], P(('job', 'dp'), 'mp'), parts along dimension 0
- grad_a: float32 [32, 12800, 16], P(('job', 'dp'), 'mp'), parts along dimension 0
- grad_b: float32 [32, 16, 5120], P(('job', 'dp'), None, 'mp'), parts along dimension 0
There are 2 independent parts, one for each index of `job`. A program takes and returns all parts, laid end to end along the dimension named above; an argument that names none is the same for every part. Nothing has to cross between parts.
Inputs may be any that keep to these rules, and one draw needn't show every extreme that they name: `segment_length_list`: in each data group the lengths sum to 2048; the largest is exactly 512. `owner_slot_adapter`: each adapter stands in exactly one slot.
All inputs are finite; a program needn't handle non-finite values.
Results may differ from a plain program's by a relative error of at most 0.0055.
Values may be sent and summed in bfloat16 or wider, within the bound.
A program may use at most 192 MiB of HBM per device.

v0:
```python
import jax
import jax.numpy as jnp
from jax import lax
from jax.sharding import PartitionSpec as P


def adapter_table(lengths, labels, count_tok, adapter_token_count):
    ends = jnp.cumsum(lengths)
    starts = ends - lengths
    position = jnp.arange(count_tok, dtype=jnp.int32)[:, None]
    inside = ((position >= starts[None, :]) & (position < ends[None, :])).astype(jnp.float32)
    label_hot = (
        labels[:, None] == jnp.arange(adapter_token_count, dtype=jnp.int32)[None, :]
    ).astype(jnp.float32)
    return jnp.dot(inside, label_hot, precision=lax.Precision.HIGHEST)


def masked(values, owner, adapter_rank_size):
    shaped = values.reshape(values.shape[0], owner.shape[1], adapter_rank_size)
    return jnp.sum(shaped * owner[:, :, None], axis=1)


def spread(vector, owner):
    return (owner.astype(jnp.bfloat16)[:, :, None] * vector[:, None, :]).reshape(
        vector.shape[0], -1
    )


def shards(
    output_gradient,
    hidden,
    down_weight_frozen,
    adapter_down_maps,
    adapter_up_maps,
    segment_length_list,
    segment_adapter_index,
    owner_slot_adapter,
    adapter_token_totals,
):
    tok_all = hidden.shape[0]
    hidden_per_shard = hidden.shape[1]
    width_per_shard = adapter_up_maps.shape[2]
    adapter_token_count = adapter_down_maps.shape[0]
    adapter_rank_size = adapter_down_maps.shape[2]
    model_place = lax.axis_index("mp")
    owner = adapter_table(
        segment_length_list[0], segment_adapter_index[0], tok_all, adapter_token_count
    )
    flattened_down_maps = jnp.transpose(adapter_down_maps, (1, 0, 2)).reshape(
        hidden_per_shard, adapter_token_count * adapter_rank_size
    )
    first_col = model_place * width_per_shard
    piece = lax.all_gather(output_gradient, "mp", axis=0, tiled=True)
    main_part = lax.dot_general(
        piece, down_weight_frozen, (((1,), (1,)), ((), ())), preferred_element_type=jnp.float32
    )
    own_cols = lax.dynamic_slice_in_dim(piece, first_col, width_per_shard, 1).astype(jnp.float32)
    combined = jnp.concatenate([main_part, own_cols], axis=1)
    main = combined[:, :hidden_per_shard]
    dy_cols = combined[:, hidden_per_shard:].astype(jnp.bfloat16)
    down_part = masked(
        jnp.dot(hidden, flattened_down_maps, preferred_element_type=jnp.float32),
        owner,
        adapter_rank_size,
    )
    flattened_up_maps = adapter_up_maps.reshape(
        adapter_token_count * adapter_rank_size, width_per_shard
    )
    up_part = masked(
        lax.dot_general(
            dy_cols, flattened_up_maps, (((1,), (1,)), ((), ())), preferred_element_type=jnp.float32
        ),
        owner,
        adapter_rank_size,
    )
    low_down, low_up = lax.psum((down_part, up_part), "mp")
    low_up = low_up.astype(jnp.bfloat16)
    low_down = low_down.astype(jnp.bfloat16)
    up_spread = spread(low_up, owner)
    down_spread = spread(low_down, owner)
    extra = lax.dot_general(
        up_spread, flattened_down_maps, (((1,), (1,)), ((), ())), preferred_element_type=jnp.float32
    )
    grad_hidden = (main + 2.0 * extra).astype(jnp.bfloat16)
    raw_a = 2.0 * jnp.dot(hidden.T, up_spread, preferred_element_type=jnp.float32)
    raw_b = 2.0 * jnp.dot(down_spread.T, dy_cols, preferred_element_type=jnp.float32)
    raw_a = jnp.transpose(
        raw_a.reshape(hidden_per_shard, adapter_token_count, adapter_rank_size), (1, 0, 2)
    )
    raw_b = raw_b.reshape(adapter_token_count, adapter_rank_size, width_per_shard)
    slot_a = jnp.take(raw_a, owner_slot_adapter, axis=0)
    slot_b = jnp.take(raw_b, owner_slot_adapter, axis=0)
    per_group = adapter_token_count // lax.axis_size("dp")
    first_slot = lax.axis_index("dp") * per_group
    owned_a, owned_b = (
        lax.psum_scatter(slot_a, "dp", scatter_dimension=0, tiled=True),
        lax.psum_scatter(slot_b, "dp", scatter_dimension=0, tiled=True),
    )
    own_slots = lax.dynamic_slice_in_dim(owner_slot_adapter, first_slot, per_group, 0)
    divisor = jnp.take(adapter_token_totals, own_slots, axis=0).astype(jnp.float32)
    grad_a = owned_a / divisor[:, None, None]
    grad_b = owned_b / divisor[:, None, None]
    return (grad_hidden, grad_a, grad_b)


def solution(mesh):
    placed = (
        P(("job", "dp", "mp"), None),
        P(("job", "dp"), "mp"),
        P("mp", None),
        P(None, "mp", None),
        P(None, None, "mp"),
        P(("job", "dp"), None),
        P(("job", "dp"), None),
        P("job"),
        P("job"),
    )
    return jax.shard_map(
        shards,
        mesh=mesh,
        in_specs=placed,
        out_specs=(
            P(("job", "dp"), "mp"),
            P(("job", "dp"), "mp", None),
            P(("job", "dp"), None, "mp"),
        ),
        check_vma=False,
    )
```

profile of v0, /device:TPU:0, one launch (start us, length us, event | category | flops | bytes accessed | tf_op | source)
XLA Modules:
  0.0 533.2 jit_solution(16480140585307534754)
XLA Ops:
  7.2 0.0 copy-start
  7.2 0.0 all-gather.2.cloned.1.call-start
  7.2 0.7 all-gather.2.cloned.1.call-update
  7.9 0.0 reduce-scatter.5.cloned.1.call-start
  8.0 0.7 copy.13
  8.7 0.1 reduce
  8.9 0.7 fusion.30
  9.5 1.1 fusion.34
  10.6 0.0 copy-start.3
  10.6 0.0 copy-done
  10.6 0.0 copy-start.7
  10.6 0.0 copy-start.2
  10.6 0.0 copy-start.8
  10.6 5.0 fusion.12
  15.6 0.0 copy-done.7
  15.6 0.1 compare_select_fusion
  15.7 0.0 copy-done.2
  15.7 0.6 gather_fusion.1
  16.4 0.1 fusion.31
  16.5 397.6 %all-gather.2.cloned.1.call-done = bf16[2048,5120]{1,0:T(8,128)(2,1)} async-done(((bf16[256,5120]{1,0:T(8,128)(2,1)}), bf16[2048,5120]{1,0:T(8,128)(2,1)}) %all-gather.2.cloned.1.call-update) | async-done | bytes 20971536 | tf_op jit(solution)/shard_map/all_gather | solution.py:53
  414.1 0.0 copy-done.8
  414.1 2.8 fusion.15
  416.9 38.9 %all-reduce.2 = (bf16[2048,16]{0,1:T(8,128)(2,1)S(1)}, bf16[2048,16]{0,1:T(8,128)(2,1)S(1)}) all-reduce(f32[2048,16]{0,1:T(8,128)S(1)} %fusion.15, f32[2048,16]{0,1:T(8,128)S(1)} %fusion.12), channel_id=1, replica_groups=mesh['job'=2,'dp'=2,'mp'=8] {'mp'}, use_global_device_ids=true, to_apply=%region_2.3 | all-reduce | flops 65536 | bytes 393216 | tf_op jit(solution)/shard_map/psum | solution.py:76
  455.8 0.0 copy-start.5
  455.8 0.0 copy-done.3
  455.8 0.1 broadcast_multiply_fusion
  455.9 0.5 copy-done.5
  456.4 2.7 fusion.18
  459.1 0.6 gather_fusion.2
  459.7 0.9 broadcast_select_fusion.1
  460.7 0.0 reduce-scatter.5.cloned.1.call-update
  460.7 0.0 reduce-scatter.3.cloned.1.call-start
  460.8 4.8 fusion.4
  465.5 1.8 copy.14
  467.4 0.0 copy-start.4
  467.4 0.0 copy-start.6
  467.4 2.1 gather_fusion
  469.5 1.4 broadcast_select_fusion
  470.9 0.0 copy-done.4
  470.9 0.0 copy-done.6
  470.9 6.6 %fusion.25 = f32[2048,1600,1]{0,1,2:T(8,128)} fusion(bf16[16,1600,16]{1,2,0:T(8,128)(2,1)S(1)} %copy-done, bf16[2048,16]{0,1:T(8,128)(2,1)S(1)} %copy-done.6, bf16[2048,16]{0,1:T(8,128)(2,1)S(1)} %copy-done.4), kind=kOutput, calls=%fused_computation.24 | convolution fusion | flops 1678245888 | bytes 14057472 | tf_op jit(solution)/shard_map/dot_general | solution.py:81
  477.5 0.0 reduce-scatter.3.cloned.1.call-update
  477.5 0.0 copy-start.1
  477.5 45.2 %fusion.1 = bf16[2048,1600]{0,1:T(8,128)(2,1)} fusion(f32[2048,1600,1]{0,1,2:T(8,128)} %fusion.25, bf16[2048,5120]{1,0:T(8,128)(2,1)} %all-gather.2.cloned.1.call-done, bf16[1600,5120]{1,0:T(8,128)(2,1)} %param.11), kind=kOutput, calls=%fused_computation.5 | convolution fusion | flops 33564262400 | bytes 57016320 | tf_op jit(solution)/shard_map/dot_general | solution.py:54
  522.7 0.0 reduce-scatter.5.cloned.1.call-done
  522.7 1.8 broadcast_divide_fusion.1
  524.5 0.0 reduce-scatter.3.cloned.1.call-done
  524.5 2.2 broadcast_divide_fusion
  526.7 0.0 copy-done.1
  (5 shorter events, 0.1 us)
Async XLA Ops:
  7.2 3.4 copy-start
  7.2 406.9 %all-gather.2.cloned.1.call-start = ((), (), s32[]{:S(2)}) async-start(), calls=%async_computation.2 | async-start | bytes 23592960 | tf_op jit(solution)/shard_map/all_gather | solution.py:53
  7.9 514.8 %reduce-scatter.5.cloned.1.call-start = ((), (), s32[]{:S(2)}) async-start(), calls=%async_computation.4 | async-start | bytes 983040 | tf_op jit(solution)/shard_map/reduce_scatter | solution.py:97
  10.6 445.2 %copy-start.3 = (bf16[2048,16]{0,1:T(8,128)(2,1)}, bf16[2048,16]{0,1:T(8,128)(2,1)S(1)}, u32[]{:S(2)}) copy-start(bf16[2048,16]{0,1:T(8,128)(2,1)S(1)} %get-tuple-element.7) | copy-start | bytes 196612
  10.6 5.0 copy-start.7
  10.6 5.1 copy-start.2
  10.6 403.5 %copy-start.8 = (bf16[16,16,640]{2,1,0:T(8,128)(2,1)S(1)}, bf16[16,16,640]{2,1,0:T(8,128)(2,1)}, u32[]{:S(2)}) copy-start(bf16[16,16,640]{2,1,0:T(8,128)(2,1)} %param.13) | copy-start | bytes 983044
  455.8 0.6 copy-start.5
  460.7 63.8 %reduce-scatter.3.cloned.1.call-start = ((), (), s32[]{:S(2)}) async-start(), calls=%async_computation.3 | async-start | bytes 2555904 | tf_op jit(solution)/shard_map/reduce_scatter | solution.py:96
  467.4 3.6 copy-start.4
  467.4 3.6 copy-start.6
  477.5 49.2 %copy-start.1 = (bf16[16,1600,16]{1,2,0:T(8,128)(2,1)S(1)}, bf16[16,1600,16]{1,2,0:T(8,128)(2,1)}, u32[]{:S(2)}) copy-start(bf16[16,1600,16]{1,2,0:T(8,128)(2,1)} %param.12) | copy-start | bytes 2457604
Sparse Core Ops, SparseCore 0:
  9.5 404.4 all-gather.1
  460.8 5.6 reduce-scatter.4
  477.6 6.7 reduce-scatter.2
where the time goes:
time: 534 us; the launch traced here: 533 us
  waiting for transfers between devices  398 us (75%)
  matrix products  68.1 us (13%)
  blocking collectives  38.9 us (7%)
  between operations  13.9 us (3%)
  other arithmetic  7.49 us (1%)
  local copies, waits for them, and re-layouts  6.45 us (1%)
    all_gather x1, waiting for transfers between devices, shards(): piece = lax.all_gather(output_gradient, 'mp', axis=0, tiled=True)  398 us
    dot_general x1, matrix products, shards(): lax.dot_general(piece, down_weight_frozen, (((1,), (1,)), ((), ())), pref...  45.2 us
    psum x1, blocking collectives, shards(): low_down, low_up = lax.psum((down_part, up_part), 'mp')  38.9 us
  transfers between devices with their start and end apart: 3, of which 1 were waited for; matrix products, arithmetic and copies ran while one was open for 14% of the time, Pallas kernels for 0%

commit v1 on v0

v1 whole, which is shorter than its diff:
```python
import functools

import jax
import jax.numpy as jnp
from jax import lax
from jax.experimental import pallas as pl
from jax.experimental.pallas import tpu as pltpu
from jax.sharding import PartitionSpec as P

MESH = pl.DeviceIdType.MESH
NT = (((1,), (1,)), ((), ()))


def adapter_table(lengths, labels, count_tok, adapter_token_count):
    ends = jnp.cumsum(lengths)
    starts = ends - lengths
    position = jnp.arange(count_tok, dtype=jnp.int32)[:, None]
    inside = ((position >= starts[None, :]) & (position < ends[None, :])).astype(jnp.float32)
    label_hot = (
        labels[:, None] == jnp.arange(adapter_token_count, dtype=jnp.int32)[None, :]
    ).astype(jnp.float32)
    return jnp.dot(inside, label_hot, precision=lax.Precision.HIGHEST)


def chunks_of(rows):
    units = rows // 16
    first = max(1, units // 8)
    rest = units - first
    parts = min(3, rest)
    sizes = [first] + [rest // parts + (1 if i < rest % parts else 0) for i in range(parts)]
    out, at = [], 0
    for size in sizes:
        out.append((at * 16, size * 16))
        at += size
    return out


def gather_kernel(
    n, rank,
    dy_ref, w_ref, ups_ref, down_ref, ids_ref, part_ref,
    gh_ref, spread_ref, low_ref, cols_ref,
    g, w_v, u, out_v, spread_v, land, low_v,
    s_up, s_dn, s_y, s_recv, s_us, s_ur, s_xs, s_xr, s_ps, s_pr, s_ls, s_lr, s_loc, s_out, s_cols,
):
    m = lax.axis_index("mp")
    h = lax.axis_index("dp")
    zs = n // 2
    z, y = m // 2, m % 2
    rows = dy_ref.shape[0]
    half = u.shape[1] // 2
    width = u.shape[2]
    units = w_v.shape[0]
    chunks = chunks_of(rows)
    up, dn, across = m + 2, m - 2, z * 2 + (1 - y)

    load_dy = pltpu.make_async_copy(
        dy_ref, g.at[pl.ds(pl.multiple_of(m * rows, 16), rows)], s_loc.at[0]
    )
    load_w = pltpu.make_async_copy(w_ref, w_v, s_loc.at[1])
    load_u = pltpu.make_async_copy(ups_ref, u.at[m], s_loc.at[2])
    load_dy.start()
    load_u.start()
    load_w.start()

    barrier = pltpu.get_barrier_semaphore()
    for k in range(1, n):
        pl.semaphore_signal(barrier, inc=1, device_id={"mp": lax.rem(m + k, n)}, device_id_type=MESH)
    pl.semaphore_signal(barrier, inc=1, device_id={"dp": 1 - h}, device_id_type=MESH)
    pl.semaphore_wait(barrier, n)

    def block_copy(b, c, sem, to):
        r0, size = chunks[c]
        at = g.at[pl.ds(pl.multiple_of(b * rows + r0, 16), size)]
        return pltpu.make_async_remote_copy(
            src_ref=at, dst_ref=at, send_sem=sem.at[b, c], recv_sem=s_recv.at[b, c],
            device_id={"mp": to}, device_id_type=MESH,
        )

    my_half = pl.ds(pl.multiple_of(h * half, 16), half)
    his_half = pl.ds(pl.multiple_of((1 - h) * half, 16), half)

    def up_copy(k):
        at = u.at[m, my_half]
        return pltpu.make_async_remote_copy(
            src_ref=at, dst_ref=at, send_sem=s_us.at[k], recv_sem=s_ur.at[k],
            device_id={"mp": lax.rem(m + k, n)}, device_id_type=MESH,
        )

    def up_landed(k):
        at = u.at[lax.rem(m + n - k, n), my_half]
        return pltpu.make_async_remote_copy(
            src_ref=at, dst_ref=at, send_sem=s_us.at[k], recv_sem=s_ur.at[k],
            device_id={"mp": lax.rem(m + k, n)}, device_id_type=MESH,
        )

    def up_pass(k, part):
        at = u.at[lax.rem(m + n - k, n), part]
        return pltpu.make_async_remote_copy(
            src_ref=at, dst_ref=at, send_sem=s_xs.at[k], recv_sem=s_xr.at[k],
            device_id={"dp": 1 - h}, device_id_type=MESH,
        )

    def part_copy(k):
        to = lax.rem(m + k, n)
        return pltpu.make_async_remote_copy(
            src_ref=part_ref.at[to], dst_ref=land.at[k], send_sem=s_ps.at[k], recv_sem=s_pr.at[k],
            device_id={"mp": to}, device_id_type=MESH,
        )

    def low_copy(k, b):
        to = lax.rem(m + k, n)
        return pltpu.make_async_remote_copy(
            src_ref=low_v.at[b], dst_ref=low_v.at[b], send_sem=s_ls.at[k], recv_sem=s_lr.at[k],
            device_id={"mp": to}, device_id_type=MESH,
        )

    def start_along(b, c, up_too, dn_too):
        @pl.when(up_too)
        def _():
            block_copy(b, c, s_up, up).start()

        @pl.when(dn_too)
        def _():
            block_copy(b, c, s_dn, dn).start()

    can_up, can_dn = z < zs - 1, z > 0
    load_u.wait()
    for k in range(1, n):
        up_copy(k).start()
    load_dy.wait()
    for c in range(len(chunks)):
        block_copy(m, c, s_y, across).start()
        start_along(m, c, can_up, can_dn)
    for k in range(1, n):
        part_copy(k).start()

    block_copy(across, 0, s_y, across).wait_recv()
    start_along(across, 0, can_up, can_dn)
    for k in range(1, n):
        up_landed(k).wait_recv()
        up_pass(k, my_half).start()
    total = part_ref[m]
    for k in range(1, n):
        part_copy(k).wait_recv()
        total = total + land[k]
    low_v[m] = total.astype(jnp.bfloat16)
    for k in range(1, n):
        low_copy(k, m).start()
    for k in range(1, n):
        up_pass(k, his_half).wait_recv()
    load_w.wait()

    def cols_copy(b):
        r = pl.ds(pl.multiple_of(b * rows, 16), rows)
        if cols_ref.shape[1] == g.shape[1]:
            return pltpu.make_async_copy(g.at[r], cols_ref.at[r], s_cols.at[b])
        c = pl.ds(pl.multiple_of(m * width, 128), width)
        return pltpu.make_async_copy(g.at[r, c], cols_ref.at[r], s_cols.at[b])

    def out_copy(b):
        r = pl.ds(pl.multiple_of(b * rows, 16), rows)
        return pltpu.make_async_copy(out_v.at[r], gh_ref.at[r], s_out.at[b])

    tile = 512
    edges = [(i, min(tile, units - i)) for i in range(0, units, tile)]

    def compute(b):
        r = pl.ds(pl.multiple_of(b * rows, 16), rows)
        cols_copy(b).start()
        val = jnp.zeros((rows, 2 * half), jnp.float32)
        for j in range(n):
            val = val + lax.dot_general(
                g[r, j * width:(j + 1) * width], u[j], NT, preferred_element_type=jnp.float32
            )
        lane = lax.broadcasted_iota(jnp.int32, (rows, 2 * half), 1) // rank
        low = jnp.where(lane == ids_ref[r], val, 0.0).astype(jnp.bfloat16)
        spread_v[r] = low
        for c0, size in edges:
            acc = lax.dot_general(
                g[r], w_v[c0:c0 + size], NT, preferred_element_type=jnp.float32
            )
            acc = acc + 2.0 * lax.dot_general(
                low, down_ref[c0:c0 + size], NT, preferred_element_type=jnp.float32
            )
            out_v[r, c0:c0 + size] = acc.astype(jnp.bfloat16)
        out_copy(b).start()

    def step(d, carry):
        lo, hi = z - d, z + d
        moving = d > 0
        lo_in, hi_in = moving & (lo >= 0), moving & (hi < zs)

        def pass_on(c, side, crosses):
            @pl.when(lo_in)
            def _():
                b = lo * 2 + side
                block_copy(b, c, s_up, across).wait_recv()
                if crosses:
                    block_copy(b, c, s_y, across).start()

                @pl.when(can_up)
                def _():
                    block_copy(b, c, s_up, up).start()

            @pl.when(hi_in)
            def _():
                b = hi * 2 + side
                block_copy(b, c, s_dn, across).wait_recv()
                if crosses:
                    block_copy(b, c, s_y, across).start()

                @pl.when(can_dn)
                def _():
                    block_copy(b, c, s_dn, dn).start()

        for c in range(1, len(chunks)):
            pass_on(c, y, True)
        pass_on(0, y, False)
        pass_on(0, 1 - y, False)

        e = d - 1

        def four(i, carry):
            lower = (i % 2) == 0
            own = i < 2
            dist = jnp.where(own, d, e)
            zz = jnp.where(lower, z - dist, z + dist)
            ok = (dist >= 0) & (zz >= 0) & (zz < zs) & (lower | (dist > 0))
            b = zz * 2 + jnp.where(own, y, 1 - y)

            @pl.when(ok)
            def _():
                @pl.when(jnp.logical_not(own))
                def _():
                    for c in range(1, len(chunks)):
                        block_copy(b, c, s_y, across).wait_recv()
                compute(b)
            return carry

        lax.fori_loop(0, 4, four, 0)
        return carry

    lax.fori_loop(0, zs + 1, step, 0)

    for k in range(1, n):
        low_copy(k, lax.rem(m + n - k, n)).wait_recv()
    low_out = pltpu.make_async_copy(low_v, low_ref, s_loc.at[0])
    spread_out = pltpu.make_async_copy(spread_v, spread_ref, s_loc.at[1])
    low_out.start()
    spread_out.start()

    for k in range(1, n):
        up_copy(k).wait_send()
        up_pass(k, my_half).wait_send()
        part_copy(k).wait_send()
        low_copy(k, m).wait_send()

    def drain(b, carry):
        bz, by = b // 2, b % 2
        for c in range(len(chunks)):
            zway = (by == y) if c else (bz >= 0)

            @pl.when(can_up & (bz <= z) & zway)
            def _():
                block_copy(b, c, s_up, up).wait_send()

            @pl.when(can_dn & (bz >= z) & zway)
            def _():
                block_copy(b, c, s_dn, dn).wait_send()

            @pl.when((by == y) & (True if c else (bz == z)))
            def _():
                block_copy(b, c, s_y, across).wait_send()
        cols_copy(b).wait()
        out_copy(b).wait()
        return carry

    lax.fori_loop(0, n, drain, 0)
    low_out.wait()
    spread_out.wait()


def gather_and_multiply(n, rank, dy, w, ups, down, ids, part):
    rows, model = dy.shape
    units = w.shape[0]
    pairs, width = ups.shape
    whole = n * rows
    cols = width if width % 128 == 0 else model
    count = len(chunks_of(rows))
    any_spec = pl.BlockSpec(memory_space=pl.ANY)
    vmem = pl.BlockSpec(memory_space=pltpu.VMEM)
    dma = pltpu.SemaphoreType.DMA
    return pl.pallas_call(
        functools.partial(gather_kernel, n, rank),
        out_shape=(
            jax.ShapeDtypeStruct((whole, units), jnp.bfloat16),
            jax.ShapeDtypeStruct((whole, pairs), jnp.bfloat16),
            jax.ShapeDtypeStruct((n, rank, rows), jnp.bfloat16),
            jax.ShapeDtypeStruct((whole, cols), jnp.bfloat16),
        ),
        in_specs=[any_spec, any_spec, any_spec, vmem, vmem, vmem],
        out_specs=(any_spec,) * 4,
        scratch_shapes=[
            pltpu.VMEM((whole, model), jnp.bfloat16),
            pltpu.VMEM((units, model), jnp.bfloat16),
            pltpu.VMEM((n, pairs, width), jnp.bfloat16),
            pltpu.VMEM((whole, units), jnp.bfloat16),
            pltpu.VMEM((whole, pairs), jnp.bfloat16),
            pltpu.VMEM((n, rank, rows), jnp.float32),
            pltpu.VMEM((n, rank, rows), jnp.bfloat16),
            dma((n, count)), dma((n, count)), dma((n, count)), dma((n, count)),
            dma((n,)), dma((n,)), dma((n,)), dma((n,)),
            dma((n,)), dma((n,)), dma((n,)), dma((n,)),
            dma((3,)), dma((n,)), dma((n,)),
        ],
        compiler_params=pltpu.CompilerParams(
            collective_id=0, has_side_effects=True, vmem_limit_bytes=60 * 1024 * 1024
        ),
        cost_estimate=pl.CostEstimate(
            flops=2 * whole * model * (units + pairs), bytes_accessed=4 * whole * model,
            transcendentals=0,
        ),
    )(dy, w, ups, down, ids, part)


def shards(
    output_gradient,
    hidden,
    down_weight_frozen,
    adapter_down_maps,
    adapter_up_maps,
    segment_length_list,
    segment_adapter_index,
    owner_slot_adapter,
    adapter_token_totals,
):
    tok_all, hidden_per_shard = hidden.shape
    rows = output_gradient.shape[0]
    n = tok_all // rows
    width = adapter_up_maps.shape[2]
    count, _, rank = adapter_down_maps.shape
    owner = adapter_table(
        segment_length_list[0], segment_adapter_index[0], tok_all, count
    )
    ids = jnp.sum(
        owner * jnp.arange(count, dtype=jnp.float32)[None, :], axis=1, keepdims=True
    ).astype(jnp.int32)
    hot = (jnp.arange(count * rank, dtype=jnp.int32)[None, :] // rank) == ids
    flat_down = jnp.transpose(adapter_down_maps, (1, 0, 2)).reshape(hidden_per_shard, count * rank)
    flat_up = adapter_up_maps.reshape(count * rank, width)
    down_all = jnp.dot(hidden, flat_down, preferred_element_type=jnp.float32)
    down_part = jnp.sum(
        jnp.where(hot, down_all, 0.0).reshape(tok_all, count, rank), axis=1
    )
    part = jnp.transpose(down_part.reshape(n, rows, rank), (0, 2, 1))
    grad_hidden, up_spread, low_down, cols = gather_and_multiply(
        n, rank, output_gradient, down_weight_frozen, flat_up, flat_down, ids, part
    )
    if cols.shape[1] != width:
        cols = lax.dynamic_slice_in_dim(cols, lax.axis_index("mp") * width, width, 1)
    low_down = jnp.transpose(low_down, (0, 2, 1)).reshape(tok_all, rank)
    down_spread = jnp.where(hot, jnp.tile(low_down, (1, count)), 0).astype(jnp.bfloat16)
    raw_a = 2.0 * lax.dot_general(
        hidden, up_spread, (((0,), (0,)), ((), ())), preferred_element_type=jnp.float32
    )
    raw_b = 2.0 * lax.dot_general(
        down_spread, cols, (((0,), (0,)), ((), ())), preferred_element_type=jnp.float32
    )
    raw_a = jnp.transpose(raw_a.reshape(hidden_per_shard, count, rank), (1, 0, 2))
    raw_b = raw_b.reshape(count, rank, width)
    slot_a = jnp.take(raw_a, owner_slot_adapter, axis=0)
    slot_b = jnp.take(raw_b, owner_slot_adapter, axis=0)
    per_group = count // lax.axis_size("dp")
    first_slot = lax.axis_index("dp") * per_group
    owned_a = lax.psum_scatter(slot_a, "dp", scatter_dimension=0, tiled=True)
    owned_b = lax.psum_scatter(slot_b, "dp", scatter_dimension=0, tiled=True)
    own_slots = lax.dynamic_slice_in_dim(owner_slot_adapter, first_slot, per_group, 0)
    divisor = jnp.take(adapter_token_totals, own_slots, axis=0).astype(jnp.float32)
    grad_a = owned_a / divisor[:, None, None]
    grad_b = owned_b / divisor[:, None, None]
    return (grad_hidden, grad_a, grad_b)


def solution(mesh):
    placed = (
        P(("job", "dp", "mp"), None),
        P(("job", "dp"), "mp"),
        P("mp", None),
        P(None, "mp", None),
        P(None, None, "mp"),
        P(("job", "dp"), None),
        P(("job", "dp"), None),
        P("job"),
        P("job"),
    )
    return jax.shard_map(
        shards,
        mesh=mesh,
        in_specs=placed,
        out_specs=(
            P(("job", "dp"), "mp"),
            P(("job", "dp"), "mp", None),
            P(("job", "dp"), None, "mp"),
        ),
        check_vma=False,
    )
```

time: 534 us -> 319 us (0.60)
  waiting for transfers between devices: 398 us -> 0.04 us
  Pallas kernels: 0 us -> 262 us
  matrix products: 68.1 us -> 13.9 us
  blocking collectives: 38.9 us -> 0 us
  local copies, waits for them, and re-layouts: 6.45 us -> 18.8 us
    all_gather x1 -> x0, waiting for transfers between devices: 398 us -> none  [shards(): piece = lax.all_gather(output_gradient, 'mp', axis=0, tiled=True)]
    pallas_call x0 -> x1, Pallas kernels: none -> 262 us  [gather_and_multiply(): pl.pallas_call(functools.partial(gather_kernel, n, rank), out_shape=(jax....]
    dot_general x6 -> x3, matrix products: 67 us -> 12.8 us  [the longest x1 5.03 us: shards(): down_all = jnp.dot(hidden, flat_down, preferred_element_type=jnp.float32)]
    psum x1 -> x0, blocking collectives: 38.9 us -> none  [shards(): low_down, low_up = lax.psum((down_part, up_part), 'mp')]
    unnamed x18 -> x7, local copies, waits for them, and re-layouts: 0.51 us -> 10.3 us
  transfers between devices with their start and end apart: 3 -> 2, of which waited for: 1 -> 0; matrix products, arithmetic and copies ran while one was open for 14% -> 7% of each run, Pallas kernels for 0% -> 0%
where the time goes in v1:
time: 319 us; the launch traced here: 318 us
  Pallas kernels  262 us (82%)
  local copies, waits for them, and re-layouts  18.8 us (6%)
  between operations  14.2 us (4%)
  matrix products  13.9 us (4%)
  other arithmetic  8.92 us (3%)
    pallas_call x1, Pallas kernels, gather_and_multiply(): pl.pallas_call(functools.partial(gather_kernel, n, rank), out_shape=(jax....  262 us
    unnamed x7, local copies, waits for them, and re-layouts  10.3 us
  transfers between devices with their start and end apart: 2, of which 0 were waited for; matrix products, arithmetic and copies ran while one was open for 7% of the time, Pallas kernels for 0%

profile of v1, /device:TPU:0, one launch (start us, length us, event | category | flops | bytes accessed | tf_op | source)
XLA Modules:
  0.0 318.1 jit_solution(16707184463623441205)
XLA Ops:
  7.2 0.0 copy-start
  7.2 0.0 copy-start.1
  7.2 0.0 reduce-scatter.5.cloned.1.call-start
  7.2 0.7 compare_select_fusion.4
  8.0 0.7 compare_and_fusion
  8.6 0.7 copy.15
  9.4 0.1 reduce
  9.5 0.7 fusion.10
  10.2 1.1 fusion.1
  11.3 2.1 copy.17.down_ref
  13.4 0.0 copy-done.1
  13.4 5.0 %compare_select_fusion.1 = f32[2048,256]{0,1:T(8,128)S(1)} fusion(bf16[1600,256]{0,1:T(8,128)(2,1)S(1)} %bitcast.40, bf16[2048,1600]{0,1:T(8,128)(2,1)} %param.10, s32[2048]{0:T(1024)S(1)} %convert_element_type.14, s32[256]{0:T(256)S(1)} %and_select_fusion.1), kind=kOutput, calls=%fused_computation.6 | convolution fusion | flops 1678770176 | bytes 9479168 | tf_op jit(solution)/shard_map/dot_general | solution.py:351
  18.5 0.1 reduce_sum.19
  18.6 0.7 copy.25
  19.2 1.3 copy.18.ids_ref
  20.6 262.0 %shard_map.112 = (bf16[2048,1600]{1,0:T(8,128)(2,1)}, bf16[2048,256]{1,0:T(8,128)(2,1)}, bf16[8,16,256]{2,1,0:T(8,128)(2,1)}, bf16[2048,640]{1,0:T(8,128)(2,1)}) custom-call(bf16[256,5120]{1,0:T(8,128)(2,1)} %dy_ref.1, bf16[1600,5120]{1,0:T(8,128)(2,1)} %w_ref.1, bf16[256,640]{1,0:T(8,128)(2,1)} %bitcast.48, bf16[1600,256]{1,0:T(8,128)(2,1)} %copy.17.down_ref, ...), custom_call_target="tpu_custom_call" | custom-call | flops 38923141120 | bytes 41943040 | tf_op jit(solution)/shard_map/pallas_call | solution.py:293
  282.6 0.8 copy.23
  283.5 0.1 tile.11
  283.6 2.8 convolution_multiply_fusion.2
  286.4 0.6 gather_fusion.2
  287.0 0.9 broadcast_select_fusion.1
  287.9 0.0 reduce-scatter.5.cloned.1.call-update
  288.0 0.2 reduce-scatter.3.cloned.1.call-start
  288.2 5.0 %fusion = f32[1600,256]{1,0:T(8,128)S(1)} fusion(bf16[2048,1600]{0,1:T(8,128)(2,1)} %param.10, bf16[2048,256]{1,0:T(8,128)(2,1)} %get-tuple-element.8), kind=kOutput, calls=%fused_computation.4 | convolution fusion | flops 1678131200 | bytes 9240576 | tf_op jit(solution)/shard_map/dot_general | solution.py:363
  293.2 0.7 copy.19
  293.9 0.7 gather_fusion
  294.6 1.5 broadcast_select_fusion
  296.1 0.0 reduce-scatter.3.cloned.1.call-update
  296.1 0.0 copy-start.2
  296.1 10.3 %copy.21 = bf16[2048,1600]{0,1:T(8,128)(2,1)} copy(bf16[2048,1600]{1,0:T(8,128)(2,1)} %get-tuple-element.14) | data formatting | bytes 13107200
  306.4 0.0 copy-done.2
  306.4 0.1 compare_select_fusion.3
  306.5 0.0 copy-done
  306.5 0.6 gather_fusion.1
  307.2 0.1 fusion.11
  307.2 0.0 reduce-scatter.5.cloned.1.call-done
  307.2 1.8 broadcast_divide_fusion.1
  309.1 0.0 reduce-scatter.3.cloned.1.call-done
  309.1 2.2 broadcast_divide_fusion
  (5 shorter events, 0.1 us)
Async XLA Ops:
  7.2 299.3 %copy-start = (s32[16]{0:T(128)S(1)}, s32[16]{0:T(128)}, u32[]{:S(2)}) copy-start(s32[16]{0:T(128)} %param.17) | copy-start | bytes 196
  7.2 6.2 %copy-start.1 = (bf16[16,1600,16]{1,2,0:T(8,128)(2,1)S(1)}, bf16[16,1600,16]{1,2,0:T(8,128)(2,1)}, u32[]{:S(2)}) copy-start(bf16[16,1600,16]{1,2,0:T(8,128)(2,1)} %param.12) | copy-start | bytes 2457604
  7.2 300.0 %reduce-scatter.5.cloned.1.call-start = ((), (), s32[]{:S(2)}) async-start(), calls=%async_computation.3 | async-start | bytes 983040 | tf_op jit(solution)/shard_map/reduce_scatter | solution.py:376
  288.0 21.1 %reduce-scatter.3.cloned.1.call-start = ((), (), s32[]{:S(2)}) async-start(), calls=%async_computation.2 | async-start | bytes 2555904 | tf_op jit(solution)/shard_map/reduce_scatter | solution.py:375
  296.1 10.3 %copy-start.2 = (s32[16]{0:T(128)S(1)}, s32[16]{0:T(128)}, u32[]{:S(2)}) copy-start(s32[16]{0:T(128)} %param.16) | copy-start | bytes 196
Sparse Core Ops, SparseCore 0:
  288.1 7.1 reduce-scatter.4
  297.6 10.3 reduce-scatter.2

commit v2 on v1

--- a/solution.py
+++ b/solution.py
@@ -24,7 +24,7 @@
 
 def chunks_of(rows):
     units = rows // 16
-    first = max(1, units // 8)
+    first = max(1, units * 3 // 16)
     rest = units - first
     parts = min(3, rest)
     sizes = [first] + [rest // parts + (1 if i < rest % parts else 0) for i in range(parts)]
@@ -36,11 +36,11 @@
 
 
 def gather_kernel(
-    n, rank,
+    n, jobs, rank,
     dy_ref, w_ref, ups_ref, down_ref, ids_ref, part_ref,
     gh_ref, spread_ref, low_ref, cols_ref,
     g, w_v, u, out_v, spread_v, land, low_v,
-    s_up, s_dn, s_y, s_recv, s_us, s_ur, s_xs, s_xr, s_ps, s_pr, s_ls, s_lr, s_loc, s_out, s_cols,
+    s_up, s_dn, s_y, s_recv, s_us, s_ur, s_ys, s_yr, s_js, s_jr, s_xs, s_xr, s_ps, s_pr, s_ls, s_lr, s_loc, s_out, s_cols,
 ):
     m = lax.axis_index("mp")
     h = lax.axis_index("dp")
@@ -48,6 +48,9 @@
     z, y = m // 2, m % 2
     rows = dy_ref.shape[0]
     half = u.shape[1] // 2
+    quarter = half // jobs
+    job = lax.axis_index("job")
+    other_job = job + 1 - 2 * (job % 2)
     width = u.shape[2]
     units = w_v.shape[0]
     chunks = chunks_of(rows)
@@ -66,7 +69,9 @@
     for k in range(1, n):
         pl.semaphore_signal(barrier, inc=1, device_id={"mp": lax.rem(m + k, n)}, device_id_type=MESH)
     pl.semaphore_signal(barrier, inc=1, device_id={"dp": 1 - h}, device_id_type=MESH)
-    pl.semaphore_wait(barrier, n)
+    if jobs == 2:
+        pl.semaphore_signal(barrier, inc=1, device_id={"job": other_job}, device_id_type=MESH)
+    pl.semaphore_wait(barrier, n + jobs - 1)
 
     def block_copy(b, c, sem, to):
         r0, size = chunks[c]
@@ -79,18 +84,34 @@
     my_half = pl.ds(pl.multiple_of(h * half, 16), half)
     his_half = pl.ds(pl.multiple_of((1 - h) * half, 16), half)
 
-    def up_copy(k):
-        at = u.at[m, my_half]
+    def quarter_at(side):
+        return pl.ds(pl.multiple_of(h * half + side * quarter, 16), quarter)
+
+    mine = quarter_at(job % 2 if jobs == 2 else 0)
+    his = quarter_at(1 - job % 2 if jobs == 2 else 0)
+
+    def origin(k, side):
+        return lax.rem(z + zs - k, zs) * 2 + side
+
+    def up_copy(k, b):
+        at = u.at[b, mine]
         return pltpu.make_async_remote_copy(
             src_ref=at, dst_ref=at, send_sem=s_us.at[k], recv_sem=s_ur.at[k],
-            device_id={"mp": lax.rem(m + k, n)}, device_id_type=MESH,
-        )
-
-    def up_landed(k):
-        at = u.at[lax.rem(m + n - k, n), my_half]
-        return pltpu.make_async_remote_copy(
-            src_ref=at, dst_ref=at, send_sem=s_us.at[k], recv_sem=s_ur.at[k],
-            device_id={"mp": lax.rem(m + k, n)}, device_id_type=MESH,
+            device_id={"mp": lax.rem(z + k, zs) * 2 + y}, device_id_type=MESH,
+        )
+
+    def up_cross(k, b):
+        at = u.at[b, mine]
+        return pltpu.make_async_remote_copy(
+            src_ref=at, dst_ref=at, send_sem=s_ys.at[k], recv_sem=s_yr.at[k],
+            device_id={"mp": across}, device_id_type=MESH,
+        )
+
+    def up_job(k, part):
+        at = u.at[lax.rem(m + n - k, n), part]
+        return pltpu.make_async_remote_copy(
+            src_ref=at, dst_ref=at, send_sem=s_js.at[k], recv_sem=s_jr.at[k],
+            device_id={"job": other_job}, device_id_type=MESH,
         )
 
     def up_pass(k, part):
@@ -125,8 +146,9 @@
 
     can_up, can_dn = z < zs - 1, z > 0
     load_u.wait()
-    for k in range(1, n):
-        up_copy(k).start()
+    for k in range(1, zs):
+        up_copy(k, m).start()
+    up_cross(0, m).start()
     load_dy.wait()
     for c in range(len(chunks)):
         block_copy(m, c, s_y, across).start()
@@ -136,8 +158,17 @@
 
     block_copy(across, 0, s_y, across).wait_recv()
     start_along(across, 0, can_up, can_dn)
-    for k in range(1, n):
-        up_landed(k).wait_recv()
+    for k in range(1, zs):
+        up_copy(k, origin(k, y)).wait_recv()
+        up_cross(k, origin(k, y)).start()
+    for k in range(zs):
+        up_cross(k, origin(k, 1 - y)).wait_recv()
+    if jobs == 2:
+        for k in range(1, n):
+            up_job(k, mine).start()
+        for k in range(1, n):
+            up_job(k, his).wait_recv()
+    for k in range(1, n):
         up_pass(k, my_half).start()
     total = part_ref[m]
     for k in range(1, n):
@@ -213,31 +244,29 @@
                 def _():
                     block_copy(b, c, s_dn, dn).start()
 
-        for c in range(1, len(chunks)):
+        def pair(dist, own):
+            def one(i, carry):
+                zz = jnp.where(i == 0, z - dist, z + dist)
+                ok = (dist >= 0) & (zz >= 0) & (zz < zs) & ((i == 0) | (dist > 0))
+                b = zz * 2 + (y if own else 1 - y)
+
+                @pl.when(ok)
+                def _():
+                    if not own:
+                        for c in range(1, len(chunks)):
+                            block_copy(b, c, s_y, across).wait_recv()
+                    compute(b)
+                return carry
+
+            lax.fori_loop(0, 2, one, 0)
+
+        for c in range(1, len(chunks) - 1):
             pass_on(c, y, True)
+        pass_on(len(chunks) - 1, y, True)
+        pair(d - 1, False)
         pass_on(0, y, False)
         pass_on(0, 1 - y, False)
-
-        e = d - 1
-
-        def four(i, carry):
-            lower = (i % 2) == 0
-            own = i < 2
-            dist = jnp.where(own, d, e)
-            zz = jnp.where(lower, z - dist, z + dist)
-            ok = (dist >= 0) & (zz >= 0) & (zz < zs) & (lower | (dist > 0))
-            b = zz * 2 + jnp.where(own, y, 1 - y)
-
-            @pl.when(ok)
-            def _():
-                @pl.when(jnp.logical_not(own))
-                def _():
-                    for c in range(1, len(chunks)):
-                        block_copy(b, c, s_y, across).wait_recv()
-                compute(b)
-            return carry
-
-        lax.fori_loop(0, 4, four, 0)
+        pair(d, True)
         return carry
 
     lax.fori_loop(0, zs + 1, step, 0)
@@ -250,10 +279,16 @@
     spread_out.start()
 
     for k in range(1, n):
-        up_copy(k).wait_send()
+        if k < zs:
+            up_copy(k, m).wait_send()
+        if jobs == 2:
+            up_job(k, mine).wait_send()
         up_pass(k, my_half).wait_send()
         part_copy(k).wait_send()
         low_copy(k, m).wait_send()
+
+    for k in range(zs):
+        up_cross(k, origin(k, y)).wait_send()
 
     def drain(b, carry):
         bz, by = b // 2, b % 2
@@ -280,7 +315,7 @@
     spread_out.wait()
 
 
-def gather_and_multiply(n, rank, dy, w, ups, down, ids, part):
+def gather_and_multiply(n, jobs, rank, dy, w, ups, down, ids, part):
     rows, model = dy.shape
     units = w.shape[0]
     pairs, width = ups.shape
@@ -291,7 +326,7 @@
     vmem = pl.BlockSpec(memory_space=pltpu.VMEM)
     dma = pltpu.SemaphoreType.DMA
     return pl.pallas_call(
-        functools.partial(gather_kernel, n, rank),
+        functools.partial(gather_kernel, n, jobs, rank),
         out_shape=(
             jax.ShapeDtypeStruct((whole, units), jnp.bfloat16),
             jax.ShapeDtypeStruct((whole, pairs), jnp.bfloat16),
@@ -311,6 +346,7 @@
             dma((n, count)), dma((n, count)), dma((n, count)), dma((n, count)),
             dma((n,)), dma((n,)), dma((n,)), dma((n,)),
             dma((n,)), dma((n,)), dma((n,)), dma((n,)),
+            dma((n,)), dma((n,)), dma((n,)), dma((n,)),
             dma((3,)), dma((n,)), dma((n,)),
         ],
         compiler_params=pltpu.CompilerParams(
@@ -354,7 +390,7 @@
     )
     part = jnp.transpose(down_part.reshape(n, rows, rank), (0, 2, 1))
     grad_hidden, up_spread, low_down, cols = gather_and_multiply(
-        n, rank, output_gradient, down_weight_frozen, flat_up, flat_down, ids, part
+        n, 2 if lax.axis_size("job") % 2 == 0 else 1, rank, output_gradient, down_weight_frozen, flat_up, flat_down, ids, part
     )
     if cols.shape[1] != width:
         cols = lax.dynamic_slice_in_dim(cols, lax.axis_index("mp") * width, width, 1)

time: 319 us -> 303 us (0.950)
  Pallas kernels: 262 us -> 245 us
    pallas_call x1, Pallas kernels: 262 us -> 245 us  [gather_and_multiply(): pl.pallas_call(functools.partial(gather_kernel, n, jobs, rank), out_shape...]
where the time goes in v2:
time: 303 us; the launch traced here: 301 us
  Pallas kernels  245 us (81%)
  local copies, waits for them, and re-layouts  18.7 us (6%)
  between operations  14.2 us (5%)
  matrix products  13.9 us (5%)
  other arithmetic  8.91 us (3%)
    pallas_call x1, Pallas kernels, gather_and_multiply(): pl.pallas_call(functools.partial(gather_kernel, n, jobs, rank), out_shape...  245 us
    unnamed x7, local copies, waits for them, and re-layouts  10.2 us
  transfers between devices with their start and end apart: 2, of which 0 were waited for; matrix products, arithmetic and copies ran while one was open for 7% of the time, Pallas kernels for 0%

profile of v2, /device:TPU:0, one launch (start us, length us, event | category | flops | bytes accessed | tf_op | source)
XLA Modules:
  0.0 301.4 jit_solution(1076547269102656591)
XLA Ops:
  7.2 0.0 copy-start
  7.2 0.0 copy-start.1
  7.2 0.0 reduce-scatter.5.cloned.1.call-start
  7.2 0.7 compare_select_fusion.4
  8.0 0.7 compare_and_fusion
  8.6 0.7 copy.15
  9.4 0.1 reduce
  9.5 0.7 fusion.10
  10.2 1.1 fusion.1
  11.3 2.1 copy.17.down_ref
  13.4 0.0 copy-done.1
  13.4 5.0 %compare_select_fusion.1 = f32[2048,256]{0,1:T(8,128)S(1)} fusion(bf16[1600,256]{0,1:T(8,128)(2,1)S(1)} %bitcast.40, bf16[2048,1600]{0,1:T(8,128)(2,1)} %param.10, s32[2048]{0:T(1024)S(1)} %convert_element_type.14, s32[256]{0:T(256)S(1)} %and_select_fusion.1), kind=kOutput, calls=%fused_computation.6 | convolution fusion | flops 1678770176 | bytes 9479168 | tf_op jit(solution)/shard_map/dot_general | solution.py:387
  18.5 0.1 reduce_sum.19
  18.6 0.7 copy.25
  19.2 1.3 copy.18.ids_ref
  20.6 245.4 %shard_map.112 = (bf16[2048,1600]{1,0:T(8,128)(2,1)}, bf16[2048,256]{1,0:T(8,128)(2,1)}, bf16[8,16,256]{2,1,0:T(8,128)(2,1)}, bf16[2048,640]{1,0:T(8,128)(2,1)}) custom-call(bf16[256,5120]{1,0:T(8,128)(2,1)} %dy_ref.1, bf16[1600,5120]{1,0:T(8,128)(2,1)} %w_ref.1, bf16[256,640]{1,0:T(8,128)(2,1)} %bitcast.48, bf16[1600,256]{1,0:T(8,128)(2,1)} %copy.17.down_ref, ...), custom_call_target="tpu_custom_call" | custom-call | flops 38923141120 | bytes 41943040 | tf_op jit(solution)/shard_map/pallas_call | solution.py:328
  266.0 0.8 copy.23
  266.9 0.1 tile.11
  267.0 2.8 convolution_multiply_fusion.2
  269.8 0.6 gather_fusion.2
  270.4 0.9 broadcast_select_fusion.1
  271.3 0.0 reduce-scatter.5.cloned.1.call-update
  271.4 0.3 reduce-scatter.3.cloned.1.call-start
  271.6 5.0 %fusion = f32[1600,256]{1,0:T(8,128)S(1)} fusion(bf16[2048,1600]{0,1:T(8,128)(2,1)} %param.10, bf16[2048,256]{1,0:T(8,128)(2,1)} %get-tuple-element.8), kind=kOutput, calls=%fused_computation.4 | convolution fusion | flops 1678131200 | bytes 9240576 | tf_op jit(solution)/shard_map/dot_general | solution.py:399
  276.6 0.7 copy.19
  277.4 0.7 gather_fusion
  278.0 1.5 broadcast_select_fusion
  279.5 0.0 reduce-scatter.3.cloned.1.call-update
  279.5 0.0 copy-start.2
  279.6 10.2 %copy.21 = bf16[2048,1600]{0,1:T(8,128)(2,1)} copy(bf16[2048,1600]{1,0:T(8,128)(2,1)} %get-tuple-element.14) | data formatting | bytes 13107200
  289.8 0.0 copy-done.2
  289.8 0.1 compare_select_fusion.3
  289.9 0.0 copy-done
  289.9 0.6 gather_fusion.1
  290.5 0.1 fusion.11
  290.6 0.0 reduce-scatter.5.cloned.1.call-done
  290.6 1.8 broadcast_divide_fusion.1
  292.4 0.0 reduce-scatter.3.cloned.1.call-done
  292.4 2.2 broadcast_divide_fusion
  (5 shorter events, 0.1 us)
Async XLA Ops:
  7.2 282.7 %copy-start = (s32[16]{0:T(128)S(1)}, s32[16]{0:T(128)}, u32[]{:S(2)}) copy-start(s32[16]{0:T(128)} %param.17) | copy-start | bytes 196
  7.2 6.2 %copy-start.1 = (bf16[16,1600,16]{1,2,0:T(8,128)(2,1)S(1)}, bf16[16,1600,16]{1,2,0:T(8,128)(2,1)}, u32[]{:S(2)}) copy-start(bf16[16,1600,16]{1,2,0:T(8,128)(2,1)} %param.12) | copy-start | bytes 2457604
  7.2 283.4 %reduce-scatter.5.cloned.1.call-start = ((), (), s32[]{:S(2)}) async-start(), calls=%async_computation.3 | async-start | bytes 983040 | tf_op jit(solution)/shard_map/reduce_scatter | solution.py:412
  271.4 21.0 %reduce-scatter.3.cloned.1.call-start = ((), (), s32[]{:S(2)}) async-start(), calls=%async_computation.2 | async-start | bytes 2555904 | tf_op jit(solution)/shard_map/reduce_scatter | solution.py:411
  279.5 10.2 %copy-start.2 = (s32[16]{0:T(128)S(1)}, s32[16]{0:T(128)}, u32[]{:S(2)}) copy-start(s32[16]{0:T(128)} %param.16) | copy-start | bytes 196
Sparse Core Ops, SparseCore 0:
  271.5 7.8 reduce-scatter.4
  281.7 10.3 reduce-scatter.2

commit v3 on v2

--- a/solution.py
+++ b/solution.py
@@ -395,7 +395,12 @@
     if cols.shape[1] != width:
         cols = lax.dynamic_slice_in_dim(cols, lax.axis_index("mp") * width, width, 1)
     low_down = jnp.transpose(low_down, (0, 2, 1)).reshape(tok_all, rank)
-    down_spread = jnp.where(hot, jnp.tile(low_down, (1, count)), 0).astype(jnp.bfloat16)
+    lanes = jnp.arange(count * rank, dtype=jnp.int32)
+    source = jnp.repeat(owner_slot_adapter, rank) * rank + lanes % rank
+    order = (lanes[:, None] == source[None, :]).astype(jnp.bfloat16)
+    up_spread = jnp.dot(up_spread, order, preferred_element_type=jnp.float32).astype(jnp.bfloat16)
+    hot_slot = ids == (source // rank)[None, :]
+    down_spread = jnp.where(hot_slot, jnp.tile(low_down, (1, count)), 0).astype(jnp.bfloat16)
     raw_a = 2.0 * lax.dot_general(
         hidden, up_spread, (((0,), (0,)), ((), ())), preferred_element_type=jnp.float32
     )
@@ -404,12 +409,10 @@
     )
     raw_a = jnp.transpose(raw_a.reshape(hidden_per_shard, count, rank), (1, 0, 2))
     raw_b = raw_b.reshape(count, rank, width)
-    slot_a = jnp.take(raw_a, owner_slot_adapter, axis=0)
-    slot_b = jnp.take(raw_b, owner_slot_adapter, axis=0)
     per_group = count // lax.axis_size("dp")
     first_slot = lax.axis_index("dp") * per_group
-    owned_a = lax.psum_scatter(slot_a, "dp", scatter_dimension=0, tiled=True)
-    owned_b = lax.psum_scatter(slot_b, "dp", scatter_dimension=0, tiled=True)
+    owned_a = lax.psum_scatter(raw_a, "dp", scatter_dimension=0, tiled=True)
+    owned_b = lax.psum_scatter(raw_b, "dp", scatter_dimension=0, tiled=True)
     own_slots = lax.dynamic_slice_in_dim(owner_slot_adapter, first_slot, per_group, 0)
     divisor = jnp.take(adapter_token_totals, own_slots, axis=0).astype(jnp.float32)
     grad_a = owned_a / divisor[:, None, None]

time: 303 us -> 301 us (level)
  other arithmetic: 8.91 us -> 5.09 us
    select_n x3 -> x1, other arithmetic: 3.15 us -> 0.01 us  [shards(): hot_slot = ids == (source // rank)[None, :]]
  transfers between devices with their start and end apart: 2 -> 2, of which waited for: 0 -> 1; matrix products, arithmetic and copies ran while one was open for 7% -> 7% of each run, Pallas kernels for 0% -> 0%
where the time goes in v3:
time: 301 us; the launch traced here: 300 us
  Pallas kernels  245 us (81%)
  local copies, waits for them, and re-layouts  18.6 us (6%)
  matrix products  15.5 us (5%)
  between operations  14.1 us (5%)
  other arithmetic  5.09 us (2%)
    pallas_call x1, Pallas kernels, gather_and_multiply(): pl.pallas_call(functools.partial(gather_kernel, n, jobs, rank), out_shape...  245 us
    unnamed x7, local copies, waits for them, and re-layouts  10.2 us
  transfers between devices with their start and end apart: 2, of which 1 were waited for; matrix products, arithmetic and copies ran while one was open for 7% of the time, Pallas kernels for 0%

profile of v3, /device:TPU:0, one launch (start us, length us, event | category | flops | bytes accessed | tf_op | source)
XLA Modules:
  0.0 299.5 jit_solution(1477821124250019727)
XLA Ops:
  7.2 0.0 copy-start
  7.2 0.0 reduce-scatter.5.cloned.1.call-start
  7.2 0.7 copy.16
  8.0 0.1 reduce
  8.1 0.7 fusion.15
  8.8 1.1 fusion.1
  9.9 2.1 copy.18.down_ref
  12.0 5.2 %convolution_select_fusion = f32[2048,256]{0,1:T(8,128)S(1)} fusion(bf16[1600,256]{0,1:T(8,128)(2,1)} %bitcast.40, bf16[2048,1600]{0,1:T(8,128)(2,1)} %param.10, s32[2048]{0:T(1024)S(1)} %convert_element_type.18, s32[256]{0:T(256)S(1)} %and_select_fusion.3), kind=kOutput, calls=%fused_computation.3 | convolution fusion | flops 1678770176 | bytes 9479168 | tf_op jit(solution)/shard_map/dot_general | solution.py:387
  17.2 0.1 reduce_sum.19
  17.4 0.7 copy.26
  18.0 1.3 copy.19.ids_ref
  19.4 0.0 copy-start.1
  19.4 245.5 %shard_map.112 = (bf16[2048,1600]{1,0:T(8,128)(2,1)}, bf16[2048,256]{1,0:T(8,128)(2,1)}, bf16[8,16,256]{2,1,0:T(8,128)(2,1)}, bf16[2048,640]{1,0:T(8,128)(2,1)}) custom-call(bf16[256,5120]{1,0:T(8,128)(2,1)} %dy_ref.1, bf16[1600,5120]{1,0:T(8,128)(2,1)} %w_ref.1, bf16[256,640]{1,0:T(8,128)(2,1)} %bitcast.48, bf16[1600,256]{1,0:T(8,128)(2,1)} %copy.18.down_ref, ...), custom_call_target="tpu_custom_call" | custom-call | flops 38923141120 | bytes 41943040 | tf_op jit(solution)/shard_map/pallas_call | solution.py:328
  264.8 0.8 copy.24
  265.7 0.0 copy-done.1
  265.7 0.1 broadcast_in_dim.13
  265.8 0.1 mul.49
  265.9 0.1 tile.11
  266.0 0.0 copy-start.2
  266.0 3.7 %convolution_multiply_fusion.2 = f32[256,640]{1,0:T(8,128)} fusion(bf16[2048,640]{1,0:T(8,128)(2,1)} %get-tuple-element.10, bf16[2048,256]{0,1:T(8,128)(2,1)S(1)} %bitcast.38, s32[2048]{0:T(1024)S(1)} %convert_element_type.18, s32[256]{0:T(256)S(1)} %get-tuple-element.17), kind=kOutput, calls=%fused_computation.7 | convolution fusion | flops 672301056 | bytes 4334592 | tf_op jit(solution)/shard_map/dot_general | solution.py:407
  269.7 0.0 reduce-scatter.5.cloned.1.call-update
  269.8 0.0 reduce-scatter.3.cloned.1.call-start
  269.8 0.0 copy-done.2
  269.8 5.5 %fusion = f32[1600,256]{1,0:T(8,128)S(1)} fusion(bf16[2048,1600]{0,1:T(8,128)(2,1)} %param.10, bf16[2048,256]{1,0:T(8,128)(2,1)S(1)} %copy-done.2, s32[256]{0:T(256)S(1)} %get-tuple-element.18), kind=kOutput, calls=%fused_computation.2 | convolution fusion | flops 1947156480 | bytes 9241600 | tf_op jit(solution)/shard_map/dot_general | solution.py:404
  275.3 1.7 copy.20
  277.0 0.0 reduce-scatter.3.cloned.1.call-update
  277.1 10.2 %copy.22 = bf16[2048,1600]{0,1:T(8,128)(2,1)} copy(bf16[2048,1600]{1,0:T(8,128)(2,1)} %get-tuple-element.14) | data formatting | bytes 13107200
  287.3 0.1 compare_select_fusion.2
  287.4 0.0 copy-done
  287.4 0.6 gather_fusion
  288.0 0.1 fusion.16
  288.1 0.0 reduce-scatter.5.cloned.1.call-done
  288.1 1.8 broadcast_divide_fusion.1
  289.9 0.6 reduce-scatter.3.cloned.1.call-done
  290.5 2.2 broadcast_divide_fusion
  (6 shorter events, 0.1 us)
Async XLA Ops:
  7.2 280.2 %copy-start = (s32[16]{0:T(128)S(1)}, s32[16]{0:T(128)}, u32[]{:S(2)}) copy-start(s32[16]{0:T(128)} %param.17) | copy-start | bytes 196
  7.2 280.9 %reduce-scatter.5.cloned.1.call-start = ((), (), s32[]{:S(2)}) async-start(), calls=%async_computation.3 | async-start | bytes 983040 | tf_op jit(solution)/shard_map/reduce_scatter | solution.py:415
  19.4 246.3 %copy-start.1 = (s32[16]{0:T(128)S(1)}, s32[16]{0:T(128)}, u32[]{:S(2)}) copy-start(s32[16]{0:T(128)} %param.16) | copy-start | bytes 196
  266.0 3.8 %copy-start.2 = (bf16[2048,256]{1,0:T(8,128)(2,1)S(1)}, bf16[2048,256]{1,0:T(8,128)(2,1)}, u32[]{:S(2)}) copy-start(bf16[2048,256]{1,0:T(8,128)(2,1)} %get-tuple-element.8) | copy-start | bytes 3145732
  269.8 20.7 %reduce-scatter.3.cloned.1.call-start = ((), (), s32[]{:S(2)}) async-start(), calls=%async_computation.2 | async-start | bytes 2555904 | tf_op jit(solution)/shard_map/reduce_scatter | solution.py:414
Sparse Core Ops, SparseCore 0:
  269.9 7.8 reduce-scatter.4
  280.1 10.3 reduce-scatter.2
